TPU v7x, 128 devices: a whole 4x4x4 slice. The times are simulated.
128 devices in a mesh: depth: 4 (over y), tile: 32 (over z, x, core).
Axes of the slice: x: 4, y: 4, z: 4, core: 2. Of those that a mesh axis runs over, the one named last changes fastest.
Arguments:
- field: float32 [128, 2048, 2048], P('depth', 'tile'), may hold values from -1 to 1
- absorb_coef: float32 [2], replicated, may hold values from 0.01 to 0.04
- color_coef: float32 [3, 4], replicated, may hold values from -1 to 1
- light: float32 [3], replicated, may hold values from -1 to 1
Outputs:
- image: float32 [4, 2048, 2048], P(None, 'tile', 'depth')
All inputs are finite; a program needn't handle non-finite values.
Results may differ from a plain program's by a relative error of at most 0.0003.
Values sent between devices are 32-bit elements; how exact they have to be, the bound alone decides.
A program may use at most 192 MiB of HBM per device.

v0:
```python
import jax
import jax.numpy as jnp
from jax import lax
from jax.sharding import PartitionSpec as P


def with_halo(value, sides, width):
    for axis, dim in sides:
        peers, length = (lax.axis_size(axis), value.shape[dim])
        up = [(i, (i + 1) % peers) for i in range(peers - 1)]
        down = [(j, i) for i, j in up]
        last = lax.slice_in_dim(value, length - width, length, axis=dim)
        initial = lax.slice_in_dim(value, 0, width, axis=dim)
        before = lax.ppermute(last, axis, up)
        after = lax.ppermute(initial, axis, down)
        value = jnp.concatenate([before, value, after], axis=dim)
    return value


def slab_light(padded, absorb_coef, color_coef, light):
    center = padded[1:-1, 1:-1]
    grad_z = 0.5 * (padded[2:, 1:-1] - padded[:-2, 1:-1])
    grad_x = 0.5 * (padded[1:-1, 2:] - padded[1:-1, :-2])
    side_pad = jnp.pad(center, ((0, 0), (0, 0), (1, 1)))
    grad_y = 0.5 * (side_pad[:, :, 2:] - side_pad[:, :, :-2])
    facing = jnp.abs(light[0] * grad_z + light[1] * grad_x + light[2] * grad_y)
    shade = facing / jnp.sqrt(grad_z * grad_z + grad_x * grad_x + grad_y * grad_y + 1.0)
    sigma = absorb_coef[0] + absorb_coef[1] * center * center
    coef = color_coef[:, :, None, None, None]
    poly = coef[:, 0] + center * (coef[:, 1] + center * (coef[:, 2] + center * coef[:, 3]))
    return (sigma, shade[None] * poly)


def over_front(front, back):
    return front + (1.0 - front[3:4]) * back


def on_device(field, absorb_coef, color_coef, light):
    padded = with_halo(field, (("depth", 0), ("tile", 1)), 1)
    sigma, emitted = slab_light(padded, absorb_coef, color_coef, light)
    running = jnp.cumsum(sigma, axis=0)
    before = running - sigma
    weight = (1.0 - jnp.exp(-sigma)) * jnp.exp(-before)
    color = jnp.sum(emitted * weight[None], axis=1)
    optical = running[-1]
    partial_image = jnp.concatenate([color, (1.0 - jnp.exp(-optical))[None]], axis=0)
    pieces = lax.all_to_all(partial_image[None], "depth", split_axis=3, concat_axis=0, tiled=True)
    total = pieces[0]
    for slab in range(1, pieces.shape[0]):
        total = over_front(total, pieces[slab])
    return total


def solution(mesh):
    in_specs = (P("depth", "tile", None), P(), P(), P())
    out_specs = P(None, "tile", "depth")
    return jax.shard_map(
        on_device, mesh=mesh, in_specs=in_specs, out_specs=out_specs, check_vma=False
    )
```

profile of v0, /device:TPU:38, one launch (start us, length us, event | category | flops | bytes accessed | tf_op | source)
XLA Modules:
  0.0 191.8 jit_solution(7068921546794885464)
XLA Ops:
  0.0 1.3 fusion.18
  1.3 3.5 %collective-permute-start.1 = (f32[1,64,2048]{2,1,0:T(8,128)S(1)}, f32[1,64,2048]{2,1,0:T(8,128)S(1)}, u32[]{:S(2)}, u32[]{:S(2)}) collective-permute-start(f32[1,64,2048]{2,1,0:T(8,128)S(1)} %get-tuple-element.14), channel_id=1, source_target_pairs={{0,32},{32,64},{64,96},{1,33},{33,65},{65,97},{2,34},{34,66},{66,9... | collective-permute-start | bytes 1572872 | tf_op jit(solution)/shard_map/ppermute | solution.py:14
  4.8 1.3 collective-permute-start
  6.1 9.8 %collective-permute-done.1 = f32[1,64,2048]{2,1,0:T(8,128)S(1)} collective-permute-done((f32[1,64,2048]{2,1,0:T(8,128)S(1)}, f32[1,64,2048]{2,1,0:T(8,128)S(1)}, u32[]{:S(2)}, u32[]{:S(2)}) %collective-permute-start.1) | collective-permute-done | bytes 524320 | tf_op jit(solution)/shard_map/ppermute | solution.py:14
  16.0 0.0 copy-start.2
  16.0 0.0 copy-start.3
  16.0 0.0 copy-start.1
  16.0 7.4 %constant_dynamic-update-slice_fusion.1 = f32[34,64,2048]{2,1,0:T(8,128)S(1)} fusion(f32[34,64,2048]{2,1,0:T(8,128)S(1)} %constant_dynamic-update-slice_fusion.2, f32[32,64,2048]{2,1,0:T(8,128)} %param.4), kind=kLoop, calls=%fused_computation.37 | loop fusion | bytes 33554432
  23.5 6.1 %copy-done = f32[34,64,2048]{2,1,0:T(8,128)} copy-done((f32[34,64,2048]{2,1,0:T(8,128)}, f32[34,64,2048]{2,1,0:T(8,128)S(1)}, u32[]{:S(2)}) %copy-start) | copy-done | bytes 17825816
  29.6 0.5 fusion.17
  30.1 1.9 %collective-permute-start.2 = (f32[34,1,2048]{2,1,0:T(1,128)S(1)}, f32[34,1,2048]{2,1,0:T(1,128)S(1)}, u32[]{:S(2)}, u32[]{:S(2)}) collective-permute-start(f32[34,1,2048]{2,1,0:T(1,128)S(1)} %get-tuple-element.9), channel_id=1, source_target_pairs={{1,0},{2,1},{3,2},{4,3},{5,4},{6,5},{7,6},{8,7},{9,8},{10,9},{11,1... | collective-permute-start | bytes 835592 | tf_op jit(solution)/shard_map/ppermute | solution.py:15
  32.1 2.4 %collective-permute-start.3 = (f32[34,1,2048]{2,1,0:T(1,128)S(1)}, f32[34,1,2048]{2,1,0:T(1,128)S(1)}, u32[]{:S(2)}, u32[]{:S(2)}) collective-permute-start(f32[34,1,2048]{2,1,0:T(1,128)S(1)} %get-tuple-element.10), channel_id=1, source_target_pairs={{0,1},{1,2},{2,3},{3,4},{4,5},{5,6},{6,7},{7,8},{8,9},{9,10},{10,1... | collective-permute-start | bytes 835592 | tf_op jit(solution)/shard_map/ppermute | solution.py:14
  34.5 0.7 fusion.20
  37.1 0.6 fusion.21
  37.7 0.2 slice_reduce_fusion.3
  37.9 2.1 %collective-permute-done.3 = f32[34,1,2048]{2,1,0:T(1,128)S(1)} collective-permute-done((f32[34,1,2048]{2,1,0:T(1,128)S(1)}, f32[34,1,2048]{2,1,0:T(1,128)S(1)}, u32[]{:S(2)}, u32[]{:S(2)}) %collective-permute-start.3) | collective-permute-done | bytes 278560 | tf_op jit(solution)/shard_map/ppermute | solution.py:14
  39.9 68.0 %rsqrt_multiply_fusion = (f32[32,64,2048]{2,1,0:T(8,128)}, f32[32,64,2048]{2,1,0:T(8,128)}, f32[32,64,2048]{2,1,0:T(8,128)}) fusion(f32[32,64,2048]{2,1,0:T(8,128)} %param.4, f32[34,64,2048]{2,1,0:T(8,128)} %copy-done, f32[34,1,2048]{2,1,0:T(1,128)S(1)} %collective-permute-done.3, f32[34,1,2048]{2,1,0:T(1,128)S(1)} %collective-permute-done.2, ...), kind=kOutput, calls=%fused_computation.13 | output fusion | flops 272629760 | bytes 103321088 | tf_op jit(solution)/shard_map/jit(cumsum)/reduce_window_sum | solution.py:41
  107.9 1.1 fusion.9
  109.1 20.6 %multiply_reduce_fusion = f32[3,64,2048]{2,1,0:T(8,128)} fusion(f32[32,64,2048]{2,1,0:T(8,128)} %get-tuple-element.12, f32[3]{0:T(128)S(1)} %get-tuple-element.6, f32[3]{0:T(128)S(1)} %get-tuple-element.7, f32[3]{0:T(128)S(1)} %get-tuple-element.8, f32[32,64,2048]{2,1,0:T(8,128)} %param.4, f32[3]{0:T(128)S(1)} %get-tuple-element.5, ...), kind=kLoop, calls=%fused_computation | loop fusion | flops 112852992 | bytes 51904560 | tf_op jit(solution)/shard_map/reduce_sum | solution.py:44
  129.6 1.6 maximum_bitcast_fusion
  131.2 3.2 %copy.13 = f32[1,4,64,2048]{2,1,0,3:T(4,128)} copy(f32[1,4,64,2048]{3,2,1,0:T(8,128)S(1)} %maximum_bitcast_fusion) | data formatting | bytes 4194304 | tf_op jit(solution)/shard_map/broadcast_in_dim | solution.py:47
  134.4 5.5 %reshape.35 = f32[4,1,131072]{2,1,0:T(1,128)S(1)} reshape(f32[2048,1,4,64]{3,2,1,0:T(4,128)} %bitcast.39) | data formatting | bytes 4194304
  139.8 32.1 %all_to_all.15 = f32[4,1,131072]{2,1,0:T(1,128)} all-to-all(f32[4,1,131072]{2,1,0:T(1,128)S(1)} %reshape.35), channel_id=1, replica_groups=mesh['depth'=4,'tile'=32] {'depth'}, dimensions={0} | all-to-all | bytes 4194304 | tf_op jit(solution)/shard_map/all_to_all | solution.py:47
  171.9 0.5 broadcast.41
  172.5 7.7 %reduce.8 = f32[4,131072]{1,0:T(4,128)S(1)} reduce(f32[4,1,131072]{2,1,0:T(1,128)} %all_to_all.15, f32[]{:T(128)} %broadcast.41), dimensions={1}, to_apply=%all_to_all.11.reduce_sub_computation | reduce | bytes 4194308 | tf_op jit(solution)/shard_map/all_to_all | solution.py:47
  180.2 4.8 %reshape.36 = f32[2048,1,4,64]{3,2,1,0:T(4,128)} reshape(f32[4,131072]{1,0:T(4,128)S(1)} %reduce.8) | data formatting | bytes 4194304
  185.0 3.7 %copy.18 = f32[1,4,64,4,512]{4,3,2,1,0:T(4,128)S(1)} copy(f32[1,4,64,4,512]{2,1,4,3,0:T(4,128)} %bitcast.40) | data formatting | bytes 4194304 | tf_op jit(solution)/shard_map/all_to_all | solution.py:47
  188.7 1.8 fusion.19
  190.4 0.1 slice_subtract_fusion.2
  190.6 0.1 fusion.13
  190.7 0.1 fusion.11
  190.9 0.9 fusion.14
  (11 shorter events, 0.1 us)
Async XLA Ops:
  1.3 14.7 %collective-permute-start.1 = (f32[1,64,2048]{2,1,0:T(8,128)S(1)}, f32[1,64,2048]{2,1,0:T(8,128)S(1)}, u32[]{:S(2)}, u32[]{:S(2)}) collective-permute-start(f32[1,64,2048]{2,1,0:T(8,128)S(1)} %get-tuple-element.14), channel_id=1, source_target_pairs={{0,32},{32,64},{64,96},{1,33},{33,65},{65,97},{2,34},{34,66},{66,9... | collective-permute-start | bytes 1572872 | tf_op jit(solution)/shard_map/ppermute | solution.py:14
  4.8 18.7 %collective-permute-start = (f32[1,64,2048]{2,1,0:T(8,128)S(1)}, f32[1,64,2048]{2,1,0:T(8,128)S(1)}, u32[]{:S(2)}, u32[]{:S(2)}) collective-permute-start(f32[1,64,2048]{2,1,0:T(8,128)S(1)} %get-tuple-element.13), channel_id=1, source_target_pairs={{32,0},{64,32},{96,64},{33,1},{65,33},{97,65},{34,2},{66,34},{98,6... | collective-permute-start | bytes 1572872 | tf_op jit(solution)/shard_map/ppermute | solution.py:15
  16.0 18.5 %copy-start.2 = (f32[3]{0:T(128)S(1)}, f32[3]{0:T(128)}, u32[]{:S(2)}) copy-start(f32[3]{0:T(128)} %param.7) | copy-start | bytes 40
  16.0 21.1 %copy-start.3 = (f32[2]{0:T(128)S(1)}, f32[2]{0:T(128)}, u32[]{:S(2)}) copy-start(f32[2]{0:T(128)} %param.5) | copy-start | bytes 28
  16.0 21.7 %copy-start.1 = (f32[3,4]{1,0:T(4,128)S(1)}, f32[3,4]{1,0:T(4,128)}, u32[]{:S(2)}) copy-start(f32[3,4]{1,0:T(4,128)} %param.6) | copy-start | bytes 148
  23.5 6.1 %copy-start = (f32[34,64,2048]{2,1,0:T(8,128)}, f32[34,64,2048]{2,1,0:T(8,128)S(1)}, u32[]{:S(2)}) copy-start(f32[34,64,2048]{2,1,0:T(8,128)S(1)} %constant_dynamic-update-slice_fusion) | copy-start | bytes 53477380
  30.1 7.7 %collective-permute-start.2 = (f32[34,1,2048]{2,1,0:T(1,128)S(1)}, f32[34,1,2048]{2,1,0:T(1,128)S(1)}, u32[]{:S(2)}, u32[]{:S(2)}) collective-permute-start(f32[34,1,2048]{2,1,0:T(1,128)S(1)} %get-tuple-element.9), channel_id=1, source_target_pairs={{1,0},{2,1},{3,2},{4,3},{5,4},{6,5},{7,6},{8,7},{9,8},{10,9},{11,1... | collective-permute-start | bytes 835592 | tf_op jit(solution)/shard_map/ppermute | solution.py:15
  32.1 7.9 %collective-permute-start.3 = (f32[34,1,2048]{2,1,0:T(1,128)S(1)}, f32[34,1,2048]{2,1,0:T(1,128)S(1)}, u32[]{:S(2)}, u32[]{:S(2)}) collective-permute-start(f32[34,1,2048]{2,1,0:T(1,128)S(1)} %get-tuple-element.10), channel_id=1, source_target_pairs={{0,1},{1,2},{2,3},{3,4},{4,5},{5,6},{6,7},{7,8},{8,9},{9,10},{10,1... | collective-permute-start | bytes 835592 | tf_op jit(solution)/shard_map/ppermute | solution.py:14
where the time goes:
time: 192 us
  other arithmetic  100 us (52%)
  local copies, waits for them, and re-layouts  36.3 us (19%)
  blocking collectives  32.1 us (17%)
  waiting for transfers between devices  11.9 us (6%)
  starting transfers between devices  9.13 us (5%)
  between operations  2.12 us (1%)
    another operation x1, other arithmetic, on_device(): running = jnp.cumsum(sigma, axis=0)  68 us
    all_to_all x1, blocking collectives, on_device(): lax.all_to_all(partial_image[None], 'depth', split_axis=3, concat_axis=0,...  32.1 us
    unnamed x13, local copies, waits for them, and re-layouts  23.9 us
    reduce_sum x1, other arithmetic, on_device(): color = jnp.sum(emitted * weight[None], axis=1)  20.6 us
    ppermute x2, waiting for transfers between devices, with_halo(): before = lax.ppermute(last, axis, up)  11.9 us
    all_to_all x1, other arithmetic, on_device(): lax.all_to_all(partial_image[None], 'depth', split_axis=3, concat_axis=0,...  7.72 us
    ppermute x2, starting transfers between devices, with_halo(): before = lax.ppermute(last, axis, up)  5.92 us
    all_to_all x2, local copies, waits for them, and re-layouts, on_device(): lax.all_to_all(partial_image[None], 'depth', split_axis=3, concat_axis=0,...  4.17 us
  transfers between devices with their start and end apart: 4, of which 2 were waited for; matrix products, arithmetic and copies ran while one was open for 5% of the time, Pallas kernels for 0%

commit v1 on v0

--- a/solution.py
+++ b/solution.py
@@ -44,7 +44,12 @@
     color = jnp.sum(emitted * weight[None], axis=1)
     optical = running[-1]
     partial_image = jnp.concatenate([color, (1.0 - jnp.exp(-optical))[None]], axis=0)
-    pieces = lax.all_to_all(partial_image[None], "depth", split_axis=3, concat_axis=0, tiled=True)
+    pieces = jnp.concatenate(
+        lax.all_to_all(
+            jnp.stack(jnp.split(partial_image[None], lax.axis_size("depth"), axis=3)), "depth", 0, 0
+        ),
+        axis=0,
+    )
     total = pieces[0]
     for slab in range(1, pieces.shape[0]):
         total = over_front(total, pieces[slab])

time: 192 us -> 165 us (0.86)
  local copies, waits for them, and re-layouts: 36.3 us -> 17.1 us
  other arithmetic: 100 us -> 92.1 us
    unnamed x13 -> x10, local copies, waits for them, and re-layouts: 23.9 us -> 13.6 us
    all_to_all x1 -> x0, other arithmetic: 7.72 us -> none  [on_device(): lax.all_to_all(partial_image[None], 'depth', split_axis=3, concat_axis=0,...]
    all_to_all x2 -> x0, local copies, waits for them, and re-layouts: 4.17 us -> none  [on_device(): lax.all_to_all(partial_image[None], 'depth', split_axis=3, concat_axis=0,...]
    broadcast_in_dim x1 -> x0, local copies, waits for them, and re-layouts: 3.17 us -> none  [on_device(): partial_image[None]]
where the time goes in v1:
time: 165 us; the launch traced here: 164 us
  other arithmetic  92.1 us (56%)
  blocking collectives  32 us (19%)
  local copies, waits for them, and re-layouts  17.1 us (10%)
  waiting for transfers between devices  11.9 us (7%)
  starting transfers between devices  9.13 us (6%)
  between operations  2.1 us (1%)
    another operation x1, other arithmetic, on_device(): running = jnp.cumsum(sigma, axis=0)  68 us
    all_to_all x1, blocking collectives, on_device(): lax.all_to_all(jnp.stack(jnp.split(partial_image[None], lax.axis_size('de...  32 us
    reduce_sum x1, other arithmetic, on_device(): color = jnp.sum(emitted * weight[None], axis=1)  21.3 us
    unnamed x10, local copies, waits for them, and re-layouts  13.6 us
    ppermute x2, waiting for transfers between devices, with_halo(): before = lax.ppermute(last, axis, up)  11.9 us
    ppermute x2, starting transfers between devices, with_halo(): before = lax.ppermute(last, axis, up)  5.92 us
  transfers between devices with their start and end apart: 4, of which 2 were waited for; matrix products, arithmetic and copies ran while one was open for 5% of the time, Pallas kernels for 0%

profile of v1, /device:TPU:38, one launch (start us, length us, event | category | flops | bytes accessed | tf_op | source)
XLA Modules:
  0.0 164.3 jit_solution(15761900933707510122)
XLA Ops:
  0.0 1.3 fusion.20
  1.3 3.5 %collective-permute-start.1 = (f32[1,64,2048]{2,1,0:T(8,128)S(1)}, f32[1,64,2048]{2,1,0:T(8,128)S(1)}, u32[]{:S(2)}, u32[]{:S(2)}) collective-permute-start(f32[1,64,2048]{2,1,0:T(8,128)S(1)} %get-tuple-element.14), channel_id=1, source_target_pairs={{0,32},{32,64},{64,96},{1,33},{33,65},{65,97},{2,34},{34,66},{66,9... | collective-permute-start | bytes 1572872 | tf_op jit(solution)/shard_map/ppermute | solution.py:14
  4.8 1.3 collective-permute-start
  6.1 9.8 %collective-permute-done.1 = f32[1,64,2048]{2,1,0:T(8,128)S(1)} collective-permute-done((f32[1,64,2048]{2,1,0:T(8,128)S(1)}, f32[1,64,2048]{2,1,0:T(8,128)S(1)}, u32[]{:S(2)}, u32[]{:S(2)}) %collective-permute-start.1) | collective-permute-done | bytes 524320 | tf_op jit(solution)/shard_map/ppermute | solution.py:14
  16.0 0.0 copy-start.2
  16.0 0.0 copy-start.3
  16.0 0.0 copy-start.1
  16.0 7.4 %constant_dynamic-update-slice_fusion.1 = f32[34,64,2048]{2,1,0:T(8,128)S(1)} fusion(f32[34,64,2048]{2,1,0:T(8,128)S(1)} %constant_dynamic-update-slice_fusion.2, f32[32,64,2048]{2,1,0:T(8,128)} %param.4), kind=kLoop, calls=%fused_computation.43 | loop fusion | bytes 33554432
  23.5 0.0 collective-permute-done
  23.5 0.0 copy-start
  23.5 6.1 %copy-done = f32[34,64,2048]{2,1,0:T(8,128)} copy-done((f32[34,64,2048]{2,1,0:T(8,128)}, f32[34,64,2048]{2,1,0:T(8,128)S(1)}, u32[]{:S(2)}) %copy-start) | copy-done | bytes 17825816
  29.6 0.5 fusion.19
  30.1 1.9 %collective-permute-start.2 = (f32[34,1,2048]{2,1,0:T(1,128)S(1)}, f32[34,1,2048]{2,1,0:T(1,128)S(1)}, u32[]{:S(2)}, u32[]{:S(2)}) collective-permute-start(f32[34,1,2048]{2,1,0:T(1,128)S(1)} %get-tuple-element.9), channel_id=1, source_target_pairs={{1,0},{2,1},{3,2},{4,3},{5,4},{6,5},{7,6},{8,7},{9,8},{10,9},{11,1... | collective-permute-start | bytes 835592 | tf_op jit(solution)/shard_map/ppermute | solution.py:15
  32.1 2.4 %collective-permute-start.3 = (f32[34,1,2048]{2,1,0:T(1,128)S(1)}, f32[34,1,2048]{2,1,0:T(1,128)S(1)}, u32[]{:S(2)}, u32[]{:S(2)}) collective-permute-start(f32[34,1,2048]{2,1,0:T(1,128)S(1)} %get-tuple-element.10), channel_id=1, source_target_pairs={{0,1},{1,2},{2,3},{3,4},{4,5},{5,6},{6,7},{7,8},{8,9},{9,10},{10,1... | collective-permute-start | bytes 835592 | tf_op jit(solution)/shard_map/ppermute | solution.py:14
  34.5 0.0 copy-done.2
  34.5 0.7 fusion.21
  37.1 0.0 copy-done.3
  37.1 0.6 fusion.22
  37.7 0.0 copy-done.1
  37.7 0.2 slice_reduce_fusion.3
  37.9 0.0 collective-permute-done.2
  37.9 2.1 %collective-permute-done.3 = f32[34,1,2048]{2,1,0:T(1,128)S(1)} collective-permute-done((f32[34,1,2048]{2,1,0:T(1,128)S(1)}, f32[34,1,2048]{2,1,0:T(1,128)S(1)}, u32[]{:S(2)}, u32[]{:S(2)}) %collective-permute-start.3) | collective-permute-done | bytes 278560 | tf_op jit(solution)/shard_map/ppermute | solution.py:14
  39.9 68.0 %rsqrt_multiply_fusion = (f32[32,64,2048]{2,1,0:T(8,128)}, f32[32,64,2048]{2,1,0:T(8,128)}, f32[32,64,2048]{2,1,0:T(8,128)}) fusion(f32[32,64,2048]{2,1,0:T(8,128)} %param.4, f32[34,64,2048]{2,1,0:T(8,128)} %copy-done, f32[34,1,2048]{2,1,0:T(1,128)S(1)} %collective-permute-done.3, f32[34,1,2048]{2,1,0:T(1,128)S(1)} %collective-permute-done.2, ...), kind=kOutput, calls=%fused_computation.13 | output fusion | flops 272629760 | bytes 103321088 | tf_op jit(solution)/shard_map/jit(cumsum)/reduce_window_sum | solution.py:41
  107.9 1.1 fusion.15
  109.1 21.3 %multiply_reduce_fusion = f32[3,64,2048]{2,1,0:T(8,128)S(1)} fusion(f32[32,64,2048]{2,1,0:T(8,128)} %get-tuple-element.12, f32[3]{0:T(128)S(1)} %get-tuple-element.6, f32[3]{0:T(128)S(1)} %get-tuple-element.7, f32[3]{0:T(128)S(1)} %get-tuple-element.8, f32[32,64,2048]{2,1,0:T(8,128)} %param.4, f32[3]{0:T(128)S(1)} %get-tuple-element.5, ...), kind=kLoop, calls=%fused_computation | loop fusion | flops 112852992 | bytes 51904560 | tf_op jit(solution)/shard_map/reduce_sum | solution.py:44
  130.3 0.2 maximum_bitcast_fusion
  130.5 0.2 slice_bitcast_fusion.7
  130.8 0.2 pad_maximum_fusion.4
  131.0 32.0 %all_to_all.5 = f32[4,1,4,64,512]{4,3,2,1,0:T(8,128)S(1)} all-to-all(f32[4,1,4,64,512]{4,3,2,1,0:T(8,128)S(1)} %pad_maximum_fusion.4), channel_id=1, replica_groups=mesh['depth'=4,'tile'=32] {'depth'}, dimensions={0} | all-to-all | bytes 4194304 | tf_op jit(solution)/shard_map/all_to_all | solution.py:48
  163.0 0.1 fusion.13
  163.2 0.2 fusion.11
  163.4 0.9 fusion.9
  (5 shorter events, 0.1 us)
Async XLA Ops:
  1.3 14.7 %collective-permute-start.1 = (f32[1,64,2048]{2,1,0:T(8,128)S(1)}, f32[1,64,2048]{2,1,0:T(8,128)S(1)}, u32[]{:S(2)}, u32[]{:S(2)}) collective-permute-start(f32[1,64,2048]{2,1,0:T(8,128)S(1)} %get-tuple-element.14), channel_id=1, source_target_pairs={{0,32},{32,64},{64,96},{1,33},{33,65},{65,97},{2,34},{34,66},{66,9... | collective-permute-start | bytes 1572872 | tf_op jit(solution)/shard_map/ppermute | solution.py:14
  4.8 18.7 %collective-permute-start = (f32[1,64,2048]{2,1,0:T(8,128)S(1)}, f32[1,64,2048]{2,1,0:T(8,128)S(1)}, u32[]{:S(2)}, u32[]{:S(2)}) collective-permute-start(f32[1,64,2048]{2,1,0:T(8,128)S(1)} %get-tuple-element.13), channel_id=1, source_target_pairs={{32,0},{64,32},{96,64},{33,1},{65,33},{97,65},{34,2},{66,34},{98,6... | collective-permute-start | bytes 1572872 | tf_op jit(solution)/shard_map/ppermute | solution.py:15
  16.0 18.5 %copy-start.2 = (f32[3]{0:T(128)S(1)}, f32[3]{0:T(128)}, u32[]{:S(2)}) copy-start(f32[3]{0:T(128)} %param.7) | copy-start | bytes 40
  16.0 21.1 %copy-start.3 = (f32[2]{0:T(128)S(1)}, f32[2]{0:T(128)}, u32[]{:S(2)}) copy-start(f32[2]{0:T(128)} %param.5) | copy-start | bytes 28
  16.0 21.7 %copy-start.1 = (f32[3,4]{1,0:T(4,128)S(1)}, f32[3,4]{1,0:T(4,128)}, u32[]{:S(2)}) copy-start(f32[3,4]{1,0:T(4,128)} %param.6) | copy-start | bytes 148
  23.5 6.1 %copy-start = (f32[34,64,2048]{2,1,0:T(8,128)}, f32[34,64,2048]{2,1,0:T(8,128)S(1)}, u32[]{:S(2)}) copy-start(f32[34,64,2048]{2,1,0:T(8,128)S(1)} %constant_dynamic-update-slice_fusion) | copy-start | bytes 53477380
  30.1 7.7 %collective-permute-start.2 = (f32[34,1,2048]{2,1,0:T(1,128)S(1)}, f32[34,1,2048]{2,1,0:T(1,128)S(1)}, u32[]{:S(2)}, u32[]{:S(2)}) collective-permute-start(f32[34,1,2048]{2,1,0:T(1,128)S(1)} %get-tuple-element.9), channel_id=1, source_target_pairs={{1,0},{2,1},{3,2},{4,3},{5,4},{6,5},{7,6},{8,7},{9,8},{10,9},{11,1... | collective-permute-start | bytes 835592 | tf_op jit(solution)/shard_map/ppermute | solution.py:15
  32.1 7.9 %collective-permute-start.3 = (f32[34,1,2048]{2,1,0:T(1,128)S(1)}, f32[34,1,2048]{2,1,0:T(1,128)S(1)}, u32[]{:S(2)}, u32[]{:S(2)}) collective-permute-start(f32[34,1,2048]{2,1,0:T(1,128)S(1)} %get-tuple-element.10), channel_id=1, source_target_pairs={{0,1},{1,2},{2,3},{3,4},{4,5},{5,6},{6,7},{7,8},{8,9},{9,10},{10,1... | collective-permute-start | bytes 835592 | tf_op jit(solution)/shard_map/ppermute | solution.py:14
